TPU v7x, 256 devices: a whole 4x4x8 slice. The times are simulated.
256 devices in a mesh: wide: 32 (over y, z), narrow: 8 (over x, core).
Axes of the slice: x: 4, y: 4, z: 8, core: 2. Of those that a mesh axis runs over, the one named last changes fastest.
Arguments:
- point_feats: bfloat16 [64, 524288], P(None, ('wide', 'narrow')), may hold values from -6 to 6
- edge_offset: float32 [3, 8388608], P(None, ('wide', 'narrow')), may hold values from -1.5 to 1.5
- edge_point: int32 [65536, 128], P(('wide', 'narrow')), may hold values from 0 to 2047
- block_fill: int32 [65536], P(('wide', 'narrow')), may hold values from 1 to 128, as said below
- block_owner: int32 [65536, 1], P(('wide', 'narrow')), may hold values from 0 to 31; in each aligned block of 256 rows (0 to 255, 256 to 511, ...) at most 16 rows name the same one
- block_cell: int32 [65536], P(('wide', 'narrow')), may hold values from 0 to 8191
- enc_in_w: bfloat16 [128, 6], replicated, may hold values from -2.5 to 2.5
- enc_in_b: float32 [128], replicated, may hold values from -3 to 3
- enc_mid_w: bfloat16 [128, 128], replicated, may hold values from -0.5 to 0.5
- enc_mid_b: float32 [128], replicated, may hold values from -3 to 3
- enc_out_w: bfloat16 [64, 128], replicated, may hold values from -0.5 to 0.5
- point_proj: bfloat16 [64, 64], replicated, may hold values from -0.75 to 0.75
- dec_in_w: bfloat16 [128, 6], replicated, may hold values from -2.5 to 2.5
- dec_in_b: float32 [128], replicated, may hold values from -3 to 3
- dec_mid_w: bfloat16 [128, 128], replicated, may hold values from -0.5 to 0.5
- dec_mid_b: float32 [128], replicated, may hold values from -3 to 3
- dec_out_w: bfloat16 [64, 128], replicated, may hold values from -0.5 to 0.5
- cell_proj: bfloat16 [64, 64], replicated, may hold values from -0.75 to 0.75
- skip_weight: float32 [64, 64], replicated, may hold values from -0.75 to 0.75
- skip_bias: float32 [64], replicated, may hold values from -3 to 3
- spectral_weight: float32 [32, 32, 32, 64, 128], P('wide', None, 'narrow'), may hold values from -0.5 to 0.5
Outputs:
- decoded: bfloat16 [64, 524288], P(None, ('wide', 'narrow'))
Inputs may be any that keep to these rules, and one draw needn't show every extreme that they name: `edge_point`: rows of a block name points of the device that holds the block. Rows r >= block_fill of a block are padding; every device holds a block with all 128 rows live. `block_owner`: the owner's narrow index is that of the device holding the block; among the 256 blocks of one device no wide index appears more than 16 times. `block_cell`: cell index within the owner's pencil of 4 x 128 / 8 x 128 cells, row-major.
All inputs are finite; a program needn't handle non-finite values.
Results may differ from a plain program's by a relative error of at most 0.0051.
Values may be sent and summed in bfloat16 or wider, within the bound.
A program may use at most 128 MiB of HBM per device.

v0:
```python
import math
import types

import jax
import jax.numpy as jnp
import numpy as np
from jax import lax
from jax.experimental import pallas as pl
from jax.experimental.pallas import tpu as pltpu
from jax.sharding import PartitionSpec as P

G = 128
M = 32
C = 64
H = 128
ROWS = 128
WIDE = 32
NARROW = 8
SLOTS = 16
ENTRIES = WIDE * SLOTS
XL = G // WIDE
YL = G // NARROW
KZ = M // NARROW
PTS = 2048
BLKS = 256
LOW = 256
HIGH = PTS // LOW
STEP_BLKS = 64
LANES = STEP_BLKS * ROWS
STEPS = BLKS // STEP_BLKS
BF = jnp.bfloat16
F32 = jnp.float32

NT = (((1,), (1,)), ((), ()))
TN = (((0,), (0,)), ((), ()))


def dot(left, right, dims=(((1,), (0,)), ((), ()))):
    return lax.dot_general(left, right, dims, preferred_element_type=F32)


def angles(positions, waves):
    return 2.0 * np.pi * (np.outer(positions, waves) % G) / G


WAVES = np.arange(M) - M // 2


def z_table():
    turn = angles(np.arange(G), WAVES)
    both = np.stack([np.cos(turn), -np.sin(turn)], axis=2)
    return np.repeat(both.reshape(G, 2 * M), C, axis=1).astype(BF)


def y_forward_table():
    turn = angles(WAVES, np.arange(G))
    return np.concatenate([np.cos(turn), np.sin(turn)], axis=0).astype(BF)


def y_inverse_table():
    turn = angles(np.arange(G), WAVES)
    return np.concatenate([np.cos(turn), np.sin(turn)], axis=0).astype(BF)


def x_forward_table():
    turn = angles(WAVES, np.arange(G))
    same = np.eye(KZ)
    halves = []
    for wave in (np.cos(turn), np.sin(turn)):
        full = np.einsum("ix,kl->ikxl", wave, same)
        full = np.repeat(full[:, None], 2, axis=1)
        halves.append(full.reshape(M * 2 * KZ, G * KZ))
    return np.concatenate(halves, axis=0).astype(BF)


def x_inverse_table():
    turn = angles(np.arange(G), WAVES)
    same = np.eye(KZ)
    cos, sin = np.cos(turn) / M**3, np.sin(turn) / M**3
    halves = []
    for first, second in ((cos, -sin), (sin, cos)):
        full = np.einsum("xis,kl->xkisl", np.stack([first, second], axis=2), same)
        halves.append(full.reshape(G * KZ, M * 2 * KZ))
    return np.concatenate(halves, axis=0).astype(BF)


def half_gelu(half):
    slope = math.sqrt(2.0 / math.pi)
    inner = half * (half * half * (8.0 * slope * 0.044715) + 2.0 * slope)
    return half + half * jnp.tanh(inner)


def turned(value):
    lane = lax.broadcasted_iota(jnp.int32, value.shape, 1)
    rolled = pltpu.roll(value, C, 1)
    return jnp.where(lane < C, -rolled, rolled)


def prepare_network(in_w, in_b, mid_w, mid_b, turned_w, first, second, second_b):
    bias = 0.5 * in_b[...]
    high = bias.astype(BF).astype(F32)
    number = lax.broadcasted_iota(jnp.int32, (H, H), 0)
    turned_w[...] = jnp.where(number == 6, high, jnp.where(number == 7, bias - high, 0.0))
    turned_w[0:6, :] = 0.5 * in_w[...].astype(F32)
    first[...] = turned_w[...].T.astype(BF)
    second[...] = (0.5 * mid_w[...].astype(F32)).astype(BF)
    second_b[...] = jnp.broadcast_to(0.5 * mid_b[...], (H, H)).T


def network(first, second, second_b, third_w, features):
    hidden = half_gelu(dot(first[:, 0:16], features)).astype(BF)
    bias = jnp.concatenate([second_b[...]] * (features.shape[1] // ROWS), axis=1)
    hidden = half_gelu(dot(second[...], hidden) + bias).astype(BF)
    return dot(third_w[...], hidden)


FILL, OWNER, META = 8, 9, C


def prepare_blocks(owner, cell, fill, blocks):
    cell_row, cell_z = cell[...] >> 7, cell[...] & (G - 1)
    coord_x = owner[...] * XL + (cell_row >> 4)
    coord_y = lax.axis_index("narrow") * YL + (cell_row & (YL - 1))
    number = lax.broadcasted_iota(jnp.int32, (2 * C, BLKS), 0)
    facts = jnp.where((number == 6) | (number == 7), 1.0, 0.0)
    rows = [(3 + i, (2.0 * at.astype(F32) + 1.0) / G - 1.0) for i, at in enumerate((coord_x, coord_y, cell_z))]
    rows += [(FILL, fill[...]), (OWNER, owner[...]), (META, cell_row), (META + 1, cell_z), (META + 2, fill[...])]
    for place, value in rows:
        facts = jnp.where(number == place, value.astype(F32), facts)
    blocks[...] = facts.T


def block_lanes():
    lane = lax.broadcasted_iota(jnp.int32, (STEP_BLKS, LANES), 1)
    return lane - lax.broadcasted_iota(jnp.int32, (STEP_BLKS, LANES), 0) * ROWS


def edge_features(offsets, facts, distance, features_ref):
    inside = jnp.where((distance >= 0) & (distance < ROWS), 1.0, 0.0).astype(BF)
    features_ref[...] = dot(facts[:, 0:16].astype(BF), inside, TN)
    features_ref[0:3, :] = offsets
    return features_ref[...].astype(BF)


def live_lanes(facts, distance):
    fill = facts[:, FILL : FILL + 1].astype(jnp.int32)
    return jnp.where((distance >= 0) & (distance < fill), 1.0, 0.0)


def chunk(step):
    return pl.ds(pl.multiple_of(step * STEP_BLKS, STEP_BLKS), STEP_BLKS)


def point_row(points):
    return jnp.concatenate([points[i : i + 1, :] for i in range(STEP_BLKS)], axis=1)


def low_onehot(row):
    low = jnp.broadcast_to((row & (LOW - 1)).astype(F32), (16, LANES)).astype(BF)
    low = jnp.concatenate([low] * (LOW // 16), axis=0)
    number = lax.broadcasted_iota(jnp.int32, (LOW, LANES), 0).astype(F32).astype(BF)
    return jnp.where(low == number, jnp.ones((), BF), jnp.zeros((), BF))


def project_points(proj, feats, grouped):
    projected = dot(proj[...], feats[...]).astype(BF)
    for high in range(HIGH):
        grouped[high * C : (high + 1) * C, :] = projected[:, high * LOW : (high + 1) * LOW]


def chunk_inputs(step, offsets, blocks, features):
    facts = blocks[chunk(step), :]
    distance = block_lanes()
    lanes = pl.ds(pl.multiple_of(step * LANES, LANES), LANES)
    return edge_features(offsets[:, lanes], facts, distance, features), live_lanes(facts, distance)


PIECES = 16
PIECE = LANES // PIECES


def pick_high(spread, high_row):
    high_row = jnp.broadcast_to(high_row, (C, high_row.shape[1]))
    picked = spread[0:C]
    for high in range(1, HIGH):
        picked = jnp.where(high_row == high, spread[high * C : (high + 1) * C], picked)
    return picked


def encode_chunk(step, offsets, points, blocks, features, grouped, layers, sums):
    first, second, second_b, third = layers
    row = point_row(points[chunk(step), :])
    high_row = row >> 8
    onehot = low_onehot(row)
    inputs, live = chunk_inputs(step, offsets, blocks, features)
    bias = jnp.concatenate([second_b[...]] * (PIECE // ROWS), axis=1)
    raw, hidden, deep, weight, spread, message = {}, {}, {}, {}, {}, {}
    for tick in range(PIECES + 5):
        at = [tick - age if 0 <= tick - age < PIECES else None for age in range(6)]
        lanes = [None if piece is None else slice(piece * PIECE, (piece + 1) * PIECE) for piece in at]
        if at[1] is not None:
            hidden[at[1]] = half_gelu(raw.pop(at[1])).astype(BF)
        if at[3] is not None:
            deep[at[3]] = half_gelu(deep[at[3]] + bias).astype(BF)
        if at[5] is not None:
            picked = pick_high(spread.pop(at[5]), high_row[:, lanes[5]])
            message[at[5]] = (weight.pop(at[5]) * picked).astype(BF)
        if at[0] is not None:
            raw[at[0]] = dot(first[:, 0:16], inputs[:, lanes[0]])
            spread[at[0]] = dot(grouped[...], onehot[:, lanes[0]])
        if at[2] is not None:
            deep[at[2]] = dot(second[...], hidden.pop(at[2]))
        if at[4] is not None:
            weight[at[4]] = dot(third[...], deep.pop(at[4]))
    messages = jnp.concatenate([message[piece] for piece in range(PIECES)], axis=1)
    sums[chunk(step), 0:C] = dot(live.astype(BF), messages, NT)


def make_placer(owner, blocks, placer):
    before = lax.broadcasted_iota(jnp.int32, (BLKS, BLKS), 0) < lax.broadcasted_iota(
        jnp.int32, (BLKS, BLKS), 1
    )
    same = blocks[:, OWNER : OWNER + 1].astype(jnp.int32) == owner[...]
    rank = jnp.sum(jnp.where(same & before, 1, 0), axis=0, keepdims=True)
    target = owner[...] * SLOTS + rank
    slot = lax.broadcasted_iota(jnp.int32, (ENTRIES, BLKS), 0)
    placer[...] = jnp.where(slot == target, 1.0, 0.0).astype(BF)


def make_picker(owner, blocks, picker):
    before = lax.broadcasted_iota(jnp.int32, (BLKS, BLKS), 1) < lax.broadcasted_iota(
        jnp.int32, (BLKS, BLKS), 0
    )
    own = blocks[:, OWNER : OWNER + 1].astype(jnp.int32)
    rank = jnp.sum(jnp.where((own == owner[...]) & before, 1, 0), axis=1, keepdims=True)
    target = own * SLOTS + rank
    slot = lax.broadcasted_iota(jnp.int32, (BLKS, ENTRIES), 1)
    picker[...] = jnp.where(slot == target, 1.0, 0.0).astype(BF)


def unpack_values(picker, returned, proj, gathered):
    values = dot(picker[...], returned[...].reshape(ENTRIES, 2 * C)).astype(BF)
    gathered[...] = dot(values[:, 0:C], proj[...], NT)


def decode_chunk(step, points, blocks, weights, gathered, totals):
    alive = jnp.sum(live_lanes(blocks[chunk(step), :], block_lanes()), axis=0, keepdims=True)
    cells = gathered[chunk(step), :]
    cells = jnp.concatenate([cells, cells], axis=1)
    cells = jnp.concatenate([cells] * (ROWS // STEP_BLKS), axis=0).T
    spread = jnp.concatenate(
        [jnp.broadcast_to(cells[0:C, i : i + 1], (C, ROWS)) for i in range(STEP_BLKS)], axis=1
    )
    message = (weights[step] * spread).astype(BF)
    row = jnp.where(alive > 0.5, point_row(points[chunk(step), :]), -1)
    high = jnp.broadcast_to((row >> 8).astype(F32), (16, LANES)).astype(BF)
    high_rows = jnp.concatenate([high] * (C // 16), axis=0)
    parts = [jnp.where(high_rows == jnp.full((), i, BF), message, jnp.zeros((), BF)) for i in range(HIGH)]
    number = lax.broadcasted_iota(jnp.int32, (16, LANES), 0)
    parts.append(jnp.where(number == row >> 8, 1.0, 0.0).astype(BF))
    totals[...] += dot(jnp.concatenate(parts, axis=0), low_onehot(row), NT)


def finish_points(totals, out):
    for high in range(HIGH):
        degree = totals[HIGH * C + high : HIGH * C + high + 1, :]
        scale = 1.0 / jnp.maximum(jnp.sqrt(degree), 1.0)
        value = totals[high * C : (high + 1) * C, :] * scale
        out[:, high * LOW : (high + 1) * LOW] = value.astype(BF)


def entry_cells(received):
    cell_row = received[:, C : C + 1].astype(F32)
    cell_z = received[:, C + 1 : C + 2].astype(F32)
    lane = lax.broadcasted_iota(jnp.int32, (16, 2 * C), 1)
    sub = lax.broadcasted_iota(jnp.int32, (16, 2 * C), 0)
    picker = jnp.where(lane == sub + C, 1.0, 0.0).astype(BF)
    rows = dot(picker, received, NT)
    return cell_row, cell_z, rows[0:1, :], rows[1:2, :]


def exchange(axis, count, source, target, send_sem, recv_sem):
    me = lax.axis_index(axis)

    def copy(ahead, peer):
        return pltpu.make_async_remote_copy(
            src_ref=source.at[peer],
            dst_ref=target.at[me],
            send_sem=send_sem.at[ahead],
            recv_sem=recv_sem.at[ahead],
            device_id={axis: peer},
            device_id_type=pl.DeviceIdType.MESH,
        )

    def each(action):
        def step(ahead, carry):
            action(copy(ahead, lax.rem(me + ahead, count)))
            return carry

        lax.fori_loop(1, count, step, 0)

    def start(ahead):
        copy(ahead, lax.rem(me + ahead, count)).start()

    def start_all():
        each(lambda one: one.start())
        target[me] = source[me]

    return start, start_all, lambda: each(lambda one: one.wait_recv()), lambda: each(lambda one: one.wait_send())


def greet():
    barrier = pltpu.get_barrier_semaphore()
    for axis, count in (("wide", WIDE), ("narrow", NARROW)):
        me = lax.axis_index(axis)

        def step(ahead, carry):
            pl.semaphore_signal(
                barrier,
                inc=1,
                device_id={axis: lax.rem(me + ahead, count)},
                device_id_type=pl.DeviceIdType.MESH,
            )
            return carry

        lax.fori_loop(1, count, step, 0)
    return lambda: pl.semaphore_wait(barrier, WIDE + NARROW - 2)


def entry_phases(received_ref, table, phases):
    cell_z = received_ref[...].reshape(ENTRIES, 2 * C)[:, C + 1 : C + 2].astype(F32)
    position = lax.broadcasted_iota(jnp.int32, (ENTRIES, G), 1).astype(F32)
    at_z = jnp.where(position == cell_z, 1.0, 0.0).astype(BF)
    phases[...] = dot(at_z, table[...]).astype(BF)


def forward_z(received_ref, table, out, own_out, latent, start):
    received = received_ref[...].reshape(ENTRIES, 2 * C)
    cell_row, cell_z, row_xy, row_z = entry_cells(received)
    same = (cell_row * G + cell_z) == (row_xy * G + row_z)
    totals = dot(jnp.where(same, 1.0, 0.0).astype(BF), received)
    scale = 1.0 / jnp.maximum(jnp.sqrt(totals[:, C + 2 : C + 3]), 1.0)
    latent[...] = totals * scale
    own = received.astype(F32) * scale
    lane = lax.broadcasted_iota(jnp.int32, own.shape, 1)
    own = jnp.where(lane < C, own, pltpu.roll(own, C, 1))
    position = lax.broadcasted_iota(jnp.int32, (ENTRIES, G), 1).astype(F32)
    at_z = jnp.where(position == cell_z, 1.0, 0.0).astype(BF)
    pencil = lax.broadcasted_iota(jnp.int32, (XL * YL, ENTRIES), 0).astype(F32)
    at_row = jnp.where(pencil == row_xy, 1.0, 0.0).astype(BF)
    width = KZ * 2 * C
    spread = jnp.concatenate([own] * KZ, axis=1)
    me = lax.axis_index("narrow")
    for ahead in FAR_FIRST + (NARROW,):
        group = lax.rem(me + ahead, NARROW)
        phases = dot(at_z, table[:, pl.ds(pl.multiple_of(group * width, width), width)])
        modes = dot(at_row, (spread * phases).astype(BF)).astype(BF)
        place = out if ahead < NARROW else own_out
        for x in range(XL):
            place[group, :, x * width : (x + 1) * width] = modes[x * YL : (x + 1) * YL, :]
        if ahead < NARROW:
            start(ahead)


def forward_y(received, table, out, columns):
    both = dot(table[...], received[...].reshape(G, XL * KZ * 2 * C))
    for j in range(XL * KZ):
        lanes = slice(j * 2 * C, (j + 1) * 2 * C)
        columns[pl.ds(j, M, stride=XL * KZ), :] = both[0:M, lanes] - turned(both[M:, lanes])
    out[...] = columns[...].astype(BF).reshape(out.shape)


def mix_x(received, forward, inverse, weight, out, left, product):
    count = M * 2 * KZ
    both = dot(forward[...], received[...].reshape(G * KZ, 2 * C))
    modes = both[0:count] - turned(both[count:])
    row = lax.broadcasted_iota(jnp.int32, (count, 2 * C), 0)
    lane = lax.broadcasted_iota(jnp.int32, (count, 2 * C), 1)
    real_row = (row // KZ) % 2 == 0
    wide = jnp.where(real_row == (lane < C), modes, pltpu.roll(modes, C, 1))
    for half in range(KZ // 2):
        keep = row % KZ == 2 * half + lane // C
        left[:, half * 2 * C : (half + 1) * 2 * C] = jnp.where(keep, wide, 0.0)
    for kx in range(M):
        rows = slice(kx * 2 * KZ, (kx + 1) * 2 * KZ)
        product[rows, :] = dot(left[rows, :].astype(BF), weight[kx])
    back = dot(inverse[...], product[...].astype(BF))
    cells = G * KZ
    out[...] = (back[0:cells] + turned(back[cells:])).astype(BF).reshape(out.shape)


def inverse_y(received, table, out, columns):
    columns[...] = received[...].reshape(M * XL * KZ, 2 * C).astype(F32)
    for j in range(XL * KZ):
        column = columns[pl.ds(j, M, stride=XL * KZ), :].astype(BF)
        both = dot(table[...], column)
        value = both[0:G] + turned(both[G:])
        out[:, :, j * 2 * C : (j + 1) * 2 * C] = value.astype(BF).reshape(NARROW, YL, 2 * C)


def inverse_z(received_ref, linear, spectra, phases, out):
    cell_row = received_ref[...].reshape(ENTRIES, 2 * C)[:, C : C + 1].astype(F32)
    pencil = lax.broadcasted_iota(jnp.int32, (ENTRIES, XL * YL), 1).astype(F32)
    at_row = jnp.where(pencil == cell_row, 1.0, 0.0).astype(BF)
    width = KZ * 2 * C
    total = jnp.zeros((ENTRIES, 2 * C), F32)
    for group in range(NARROW):
        pencils = jnp.concatenate(
            [spectra[group, :, x * width : (x + 1) * width] for x in range(XL)], axis=0
        )
        terms = phases[:, group * width : (group + 1) * width].astype(F32) * dot(at_row, pencils)
        for j in range(KZ):
            total += terms[:, j * 2 * C : (j + 1) * 2 * C]
    spectral = total[:, 0:C] + total[:, C:]
    field = half_gelu(0.5 * (spectral + linear[...]))
    field = jnp.concatenate([field, jnp.zeros_like(field)], axis=1)
    out[...] = field.astype(BF).reshape(out.shape)


FAR_FIRST = (4, 3, 5, 2, 6, 1, 7)
WIDE_BUFFER = (WIDE, SLOTS, 2 * C)
NARROW_BUFFER = (NARROW, YL, XL * KZ * 2 * C)
WIDTH = XL * KZ * 2 * C

I32 = jnp.int32
NETWORK = dict(in_w=((6, H), BF), in_b=((1, H), F32), mid_w=((H, H), BF), mid_b=((1, H), F32), out_w=((C, H), BF))
LAYERS = dict(turned_w=((H, H), F32), first=((H, H), BF), second=((H, H), BF), second_b=((H, ROWS), F32))
BLOCK_INPUTS = dict(
    owner=((1, BLKS), I32),
    cell=((1, BLKS), I32),
    fill=((1, BLKS), I32),
    feats=((C, PTS), BF),
    point_proj=((C, C), BF),
)
EDGE_INPUTS = dict(offsets=((3, BLKS * ROWS), F32), points=((BLKS, ROWS), I32))
GRID_INPUTS = dict(
    cell_proj=((C, C), BF),
    skip=((C, C), F32),
    skip_b=((1, C), F32),
    table_z=((G, M * 2 * C), BF),
    forward_y=((2 * M, G), BF),
    forward_x=((4 * M * KZ, G * KZ), BF),
    inverse_x=((2 * G * KZ, 2 * M * KZ), BF),
    inverse_y=((2 * G, M), BF),
    spectral=((M, KZ, C, 2 * C), F32),
)
SCRATCH = dict(
    sent=(WIDE_BUFFER, BF),
    entries=(WIDE_BUFFER, BF),
    pencils=(NARROW_BUFFER, BF),
    columns=(NARROW_BUFFER, BF),
    y_modes=(WIDE_BUFFER, BF),
    slabs=(WIDE_BUFFER, BF),
    mixed=(WIDE_BUFFER, BF),
    rows=(WIDE_BUFFER, BF),
    grid=(NARROW_BUFFER, BF),
    spectra=(NARROW_BUFFER, BF),
    reply=(WIDE_BUFFER, BF),
    returned=(WIDE_BUFFER, BF),
    work=((M * XL * KZ, 2 * C), F32),
    latent=((ENTRIES, 2 * C), F32),
    linear=((ENTRIES, C), F32),
    phases=((ENTRIES, M * 2 * C), BF),
    left=((M * 2 * KZ, KZ * C), F32),
    product=((M * 2 * KZ, 2 * C), F32),
    mixer=((M, KZ * C, 2 * C), BF),
    grouped=((HIGH * C, LOW), BF),
    sums=((BLKS, 2 * C), F32),
    blocks=((BLKS, 2 * C), F32),
    placer=((ENTRIES, BLKS), BF),
    picker=((BLKS, ENTRIES), BF),
    features=((16, LANES), F32),
    weights=((STEPS, C, LANES), F32),
    gathered=((BLKS, C), F32),
    totals=((HIGH * C + 16, LOW), F32),
)
INPUT_GROUPS = (BLOCK_INPUTS, NETWORK, EDGE_INPUTS, NETWORK, GRID_INPUTS)
INPUTS = [item for group in INPUT_GROUPS for item in group.values()]
SCRATCH_GROUPS = INPUT_GROUPS + (LAYERS, LAYERS, SCRATCH)


def whole_body(*refs):
    count = len(INPUTS)
    out = refs[count]
    in_sem, wide_send, wide_recv, narrow_send, narrow_recv = refs[-5:]
    rest = iter(refs[count + 1 : -5])
    held = [types.SimpleNamespace(**{name: next(rest) for name in group}) for group in SCRATCH_GROUPS]
    block, enc, edge, dec, grid, enc_layers, dec_layers, v = held
    places = refs[count + 1 : 2 * count + 1]
    copies = [pltpu.make_async_copy(refs[i], places[i], in_sem.at[i]) for i in range(count)]
    ends = np.cumsum([len(group) for group in INPUT_GROUPS])
    for one in copies[: ends[2]]:
        one.start()
    all_in = greet()

    def need(low, high):
        for one in copies[low:high]:
            one.wait()

    def layers(raw, made):
        prepare_network(
            raw.in_w, raw.in_b, raw.mid_w, raw.mid_b, made.turned_w, made.first, made.second, made.second_b
        )
        return made.first, made.second, made.second_b, raw.out_w

    need(0, ends[1])
    prepare_blocks(block.owner, block.cell, block.fill, v.blocks)
    v.sums[...] = v.blocks[...]
    encoder = layers(enc, enc_layers)
    project_points(block.point_proj, block.feats, v.grouped)
    make_placer(block.owner, v.blocks, v.placer)
    need(ends[1], ends[2])
    for one in copies[ends[2] :]:
        one.start()

    def encode(step, carry):
        encode_chunk(step, edge.offsets, edge.points, v.blocks, v.features, v.grouped, encoder, v.sums)
        return carry

    lax.fori_loop(0, STEPS, encode, 0)
    v.sent[...] = dot(v.placer[...], v.sums[...].astype(BF)).astype(BF).reshape(v.sent.shape)
    all_in()

    def wide(number, source, target):
        return exchange("wide", WIDE, source, target, wide_send.at[number], wide_recv.at[number])

    def narrow(number, source, target):
        return exchange("narrow", NARROW, source, target, narrow_send.at[number], narrow_recv.at[number])

    _, start, receive, finish_entries = wide(0, v.sent, v.entries)
    start()
    need(ends[2], ends[4])
    decoder = layers(dec, dec_layers)

    def weigh(low, high):
        def step_body(step, carry):
            inputs, _ = chunk_inputs(step, edge.offsets, v.blocks, v.features)
            v.weights[step] = network(*decoder, inputs)
            return carry

        lax.fori_loop(low, high, step_body, 0)

    weigh(0, 1)
    receive()

    start_one, _, receive, finish_pencils = narrow(0, v.pencils, v.columns)
    forward_z(v.entries, grid.table_z, v.pencils, v.columns, v.latent, start_one)
    finish_entries()
    linear = jnp.dot(
        v.latent[:, 0:C], grid.skip[...], precision=lax.Precision.HIGHEST, preferred_element_type=F32
    )
    v.linear[...] = linear + grid.skip_b[...]
    weigh(1, 2)
    receive()

    forward_y(v.columns, grid.forward_y, v.y_modes, v.work)
    _, start, receive, finish_modes = wide(1, v.y_modes, v.slabs)
    start()
    finish_pencils()
    v.mixer[...] = grid.spectral[...].reshape(M, KZ * C, 2 * C).astype(BF)
    weigh(2, 3)
    receive()

    mix_x(v.slabs, grid.forward_x, grid.inverse_x, v.mixer, v.mixed, v.left, v.product)
    _, start, receive, finish_mixed = wide(2, v.mixed, v.rows)
    start()
    finish_modes()
    entry_phases(v.entries, grid.table_z, v.phases)
    make_picker(block.owner, v.blocks, v.picker)
    receive()

    inverse_y(v.rows, grid.inverse_y, v.grid, v.work)
    start_one, _, receive, finish_grid = narrow(1, v.grid, v.spectra)
    for ahead in FAR_FIRST:
        start_one(ahead)
    narrow_here = lax.axis_index("narrow")
    v.spectra[narrow_here] = v.grid[narrow_here]
    finish_mixed()
    weigh(3, STEPS)
    receive()

    inverse_z(v.entries, v.linear, v.spectra, v.phases, v.reply)
    _, start, receive, finish_reply = wide(3, v.reply, v.returned)
    start()
    finish_grid()
    v.totals[...] = jnp.zeros_like(v.totals)
    receive()
    unpack_values(v.picker, v.returned, grid.cell_proj, v.gathered)

    def decode(step, carry):
        decode_chunk(step, edge.points, v.blocks, v.weights, v.gathered, v.totals)
        return carry

    lax.fori_loop(0, STEPS, decode, 0)
    finish_points(v.totals, out)
    finish_reply()


def whole_call():
    scratch = [item for group in SCRATCH_GROUPS for item in group.values()]
    return pl.pallas_call(
        whole_body,
        out_shape=jax.ShapeDtypeStruct((C, PTS), BF),
        in_specs=[pl.BlockSpec(memory_space=pl.ANY)] * len(INPUTS),
        out_specs=pl.BlockSpec(memory_space=pltpu.VMEM),
        scratch_shapes=[pltpu.VMEM(shape, kind) for shape, kind in scratch]
        + [
            pltpu.SemaphoreType.DMA((len(INPUTS),)),
            pltpu.SemaphoreType.DMA((4, WIDE)),
            pltpu.SemaphoreType.DMA((4, WIDE)),
            pltpu.SemaphoreType.DMA((2, NARROW)),
            pltpu.SemaphoreType.DMA((2, NARROW)),
        ],
        compiler_params=pltpu.CompilerParams(
            collective_id=0, has_side_effects=True, vmem_limit_bytes=60 * 1024 * 1024
        ),
        name="whole",
    )


def shards(
    point_feats,
    edge_offset,
    edge_point,
    block_fill,
    block_owner,
    block_cell,
    enc_in_w,
    enc_in_b,
    enc_mid_w,
    enc_mid_b,
    enc_out_w,
    point_proj,
    dec_in_w,
    dec_in_b,
    dec_mid_w,
    dec_mid_b,
    dec_out_w,
    cell_proj,
    skip_weight,
    skip_bias,
    spectral_weight,
):
    tables = (z_table(), y_forward_table(), x_forward_table(), x_inverse_table(), y_inverse_table())
    return whole_call()(
        block_owner.reshape(1, BLKS),
        block_cell[None, :],
        block_fill[None, :],
        point_feats,
        point_proj,
        enc_in_w.T,
        enc_in_b[None, :],
        enc_mid_w,
        enc_mid_b[None, :],
        enc_out_w,
        edge_offset,
        edge_point,
        dec_in_w.T,
        dec_in_b[None, :],
        dec_mid_w,
        dec_mid_b[None, :],
        dec_out_w,
        cell_proj,
        skip_weight,
        skip_bias[None, :],
        *[jnp.asarray(table) for table in tables],
        spectral_weight[0],
    )


def solution(mesh):
    return jax.shard_map(
        shards,
        mesh=mesh,
        in_specs=(
            P(None, ("wide", "narrow")),
            P(None, ("wide", "narrow")),
            P(("wide", "narrow"), None),
            P(("wide", "narrow")),
            P(("wide", "narrow"), None),
            P(("wide", "narrow")),
            P(),
            P(),
            P(),
            P(),
            P(),
            P(),
            P(),
            P(),
            P(),
            P(),
            P(),
            P(),
            P(),
            P(),
            P("wide", None, "narrow", None, None),
        ),
        out_specs=P(None, ("wide", "narrow")),
        check_vma=False,
    )
```

profile of v0, /device:TPU:1, one launch (start us, length us, event | category | flops | bytes accessed | tf_op | source)
XLA Modules:
  0.0 90.9 jit_solution(14584961175231456363)
XLA Ops:
  0.0 89.2 %whole.1 = bf16[64,2048]{1,0:T(8,128)(2,1)} custom-call(s32[1,256]{1,0:T(1,128)} %bitcast.14, s32[1,256]{1,0:T(1,128)} %bitcast.15, s32[1,256]{1,0:T(1,128)} %bitcast.16, bf16[64,2048]{1,0:T(8,128)(2,1)} %refs_3_.1, bf16[64,64]{1,0:T(8,128)(2,1)} %refs_4_.1, bf16[6,128]{1,0:T(8,128)(2,1)} %bitcast.12, f32[1,128]{1,0:T(1,128)} %bitcast.17, ...), custom_call_target="tpu_custom_call" | custom-call | tf_op jit(solution)/shard_map/whole/pallas_call | solution.py:645
  89.2 1.7 %copy.28 = bf16[64,2048]{1,0:T(8,128)(2,1)} copy(bf16[64,2048]{1,0:T(8,128)(2,1)} %whole.1) | data formatting | bytes 524288
where the time goes:
time: 91 us; the launch traced here: 90.9 us
  Pallas kernels  89.2 us (98%)
  local copies, waits for them, and re-layouts  1.67 us (2%)
    pallas_call x1, Pallas kernels, shards(): whole_call()  89.2 us

commit v1 on v0

--- a/solution.py
+++ b/solution.py
@@ -302,11 +302,15 @@
     def start(ahead):
         copy(ahead, lax.rem(me + ahead, count)).start()
 
+    def arrive(ahead):
+        copy(ahead, lax.rem(me + ahead, count)).wait_recv()
+
     def start_all():
         each(lambda one: one.start())
         target[me] = source[me]
 
-    return start, start_all, lambda: each(lambda one: one.wait_recv()), lambda: each(lambda one: one.wait_send())
+    finish = lambda: each(lambda one: one.wait_send())
+    return start, start_all, arrive, lambda: each(lambda one: one.wait_recv()), finish
 
 
 def greet():
@@ -381,9 +385,13 @@
     for half in range(KZ // 2):
         keep = row % KZ == 2 * half + lane // C
         left[:, half * 2 * C : (half + 1) * 2 * C] = jnp.where(keep, wide, 0.0)
-    for kx in range(M):
-        rows = slice(kx * 2 * KZ, (kx + 1) * 2 * KZ)
-        product[rows, :] = dot(left[rows, :].astype(BF), weight[kx])
+    step = 4 * KZ
+    for pair in range(M // 2):
+        both = dot(left[pair * step : (pair + 1) * step, :].astype(BF), weight[pair])
+        for side in range(2):
+            rows = slice(side * 2 * KZ, (side + 1) * 2 * KZ)
+            place = pl.ds(pair * step + side * 2 * KZ, 2 * KZ)
+            product[place, :] = both[rows, side * 2 * C : (side + 1) * 2 * C]
     back = dot(inverse[...], product[...].astype(BF))
     cells = G * KZ
     out[...] = (back[0:cells] + turned(back[cells:])).astype(BF).reshape(out.shape)
@@ -398,17 +406,22 @@
         out[:, :, j * 2 * C : (j + 1) * 2 * C] = value.astype(BF).reshape(NARROW, YL, 2 * C)
 
 
-def inverse_z(received_ref, linear, spectra, phases, out):
+def inverse_z(received_ref, linear, spectra, phases, out, arrive):
     cell_row = received_ref[...].reshape(ENTRIES, 2 * C)[:, C : C + 1].astype(F32)
     pencil = lax.broadcasted_iota(jnp.int32, (ENTRIES, XL * YL), 1).astype(F32)
     at_row = jnp.where(pencil == cell_row, 1.0, 0.0).astype(BF)
     width = KZ * 2 * C
     total = jnp.zeros((ENTRIES, 2 * C), F32)
-    for group in range(NARROW):
+    me = lax.axis_index("narrow")
+    for ahead in (0,) + FAR_FIRST[::-1]:
+        if ahead > 0:
+            arrive(ahead)
+        group = lax.rem(me - ahead + NARROW, NARROW)
         pencils = jnp.concatenate(
             [spectra[group, :, x * width : (x + 1) * width] for x in range(XL)], axis=0
         )
-        terms = phases[:, group * width : (group + 1) * width].astype(F32) * dot(at_row, pencils)
+        turn = phases[:, pl.ds(pl.multiple_of(group * width, width), width)]
+        terms = turn.astype(F32) * dot(at_row, pencils)
         for j in range(KZ):
             total += terms[:, j * 2 * C : (j + 1) * 2 * C]
     spectral = total[:, 0:C] + total[:, C:]
@@ -463,7 +476,7 @@
     phases=((ENTRIES, M * 2 * C), BF),
     left=((M * 2 * KZ, KZ * C), F32),
     product=((M * 2 * KZ, 2 * C), F32),
-    mixer=((M, KZ * C, 2 * C), BF),
+    mixer=((M // 2, KZ * C, 4 * C), BF),
     grouped=((HIGH * C, LOW), BF),
     sums=((BLKS, 2 * C), F32),
     blocks=((BLKS, 2 * C), F32),
@@ -527,7 +540,7 @@
     def narrow(number, source, target):
         return exchange("narrow", NARROW, source, target, narrow_send.at[number], narrow_recv.at[number])
 
-    _, start, receive, finish_entries = wide(0, v.sent, v.entries)
+    _, start, _, receive, finish_entries = wide(0, v.sent, v.entries)
     start()
     need(ends[2], ends[4])
     decoder = layers(dec, dec_layers)
@@ -543,7 +556,7 @@
     weigh(0, 1)
     receive()
 
-    start_one, _, receive, finish_pencils = narrow(0, v.pencils, v.columns)
+    start_one, _, _, receive, finish_pencils = narrow(0, v.pencils, v.columns)
     forward_z(v.entries, grid.table_z, v.pencils, v.columns, v.latent, start_one)
     finish_entries()
     linear = jnp.dot(
@@ -554,15 +567,17 @@
     receive()
 
     forward_y(v.columns, grid.forward_y, v.y_modes, v.work)
-    _, start, receive, finish_modes = wide(1, v.y_modes, v.slabs)
+    _, start, _, receive, finish_modes = wide(1, v.y_modes, v.slabs)
     start()
     finish_pencils()
-    v.mixer[...] = grid.spectral[...].reshape(M, KZ * C, 2 * C).astype(BF)
+    mixer = grid.spectral[...].reshape(M // 2, 2, KZ * C, 2 * C).astype(BF)
+    v.mixer[:, :, 0 : 2 * C] = mixer[:, 0]
+    v.mixer[:, :, 2 * C :] = mixer[:, 1]
     weigh(2, 3)
     receive()
 
     mix_x(v.slabs, grid.forward_x, grid.inverse_x, v.mixer, v.mixed, v.left, v.product)
-    _, start, receive, finish_mixed = wide(2, v.mixed, v.rows)
+    _, start, _, receive, finish_mixed = wide(2, v.mixed, v.rows)
     start()
     finish_modes()
     entry_phases(v.entries, grid.table_z, v.phases)
@@ -570,17 +585,16 @@
     receive()
 
     inverse_y(v.rows, grid.inverse_y, v.grid, v.work)
-    start_one, _, receive, finish_grid = narrow(1, v.grid, v.spectra)
+    start_one, _, arrive, _, finish_grid = narrow(1, v.grid, v.spectra)
     for ahead in FAR_FIRST:
         start_one(ahead)
     narrow_here = lax.axis_index("narrow")
     v.spectra[narrow_here] = v.grid[narrow_here]
     finish_mixed()
     weigh(3, STEPS)
-    receive()
-
-    inverse_z(v.entries, v.linear, v.spectra, v.phases, v.reply)
-    _, start, receive, finish_reply = wide(3, v.reply, v.returned)
+
+    inverse_z(v.entries, v.linear, v.spectra, v.phases, v.reply, arrive)
+    _, start, _, receive, finish_reply = wide(3, v.reply, v.returned)
     start()
     finish_grid()
     v.totals[...] = jnp.zeros_like(v.totals)

time: 91 us -> 91.7 us (level)
  no operation moved by 1% of the time
where the time goes in v1:
time: 91.7 us; the launch traced here: 91.6 us
  Pallas kernels  89.9 us (98%)
  local copies, waits for them, and re-layouts  1.67 us (2%)
    pallas_call x1, Pallas kernels, shards(): whole_call()  89.9 us

profile of v1, /device:TPU:1, one launch (start us, length us, event | category | flops | bytes accessed | tf_op | source)
XLA Modules:
  0.0 91.6 jit_solution(15443480640010509206)
XLA Ops:
  0.0 89.9 %whole.1 = bf16[64,2048]{1,0:T(8,128)(2,1)} custom-call(s32[1,256]{1,0:T(1,128)} %bitcast.14, s32[1,256]{1,0:T(1,128)} %bitcast.15, s32[1,256]{1,0:T(1,128)} %bitcast.16, bf16[64,2048]{1,0:T(8,128)(2,1)} %refs_3_.1, bf16[64,64]{1,0:T(8,128)(2,1)} %refs_4_.1, bf16[6,128]{1,0:T(8,128)(2,1)} %bitcast.12, f32[1,128]{1,0:T(1,128)} %bitcast.17, ...), custom_call_target="tpu_custom_call" | custom-call | tf_op jit(solution)/shard_map/whole/pallas_call | solution.py:659
  89.9 1.7 %copy.28 = bf16[64,2048]{1,0:T(8,128)(2,1)} copy(bf16[64,2048]{1,0:T(8,128)(2,1)} %whole.1) | data formatting | bytes 524288
